TPU v7x, 256 devices: a whole 4x4x8 slice. The times are simulated.
256 devices in a mesh: oct: 8 (over y, core), leaf: 32 (over z, x).
Axes of the slice: x: 4, y: 4, z: 8, core: 2. Of those that a mesh axis runs over, the one named last changes fastest.
Arguments:
- probes: bfloat16 [64, 1048576], P(None, ('oct', 'leaf')), may hold values from -6 to 6
- offsets: bfloat16 [3, 1048576], P(None, ('oct', 'leaf')), may hold values from 0 to 1
- leaf_basis: bfloat16 [131072, 512], P(('oct', 'leaf')), may hold values from -0.75 to 0.75
- dev_transfer: float32 [16384, 512], P(('oct', 'leaf')), may hold values from -0.25 to 0.25
- oct_transfer: float32 [16384, 64], P(('oct', 'leaf')), may hold values from -0.75 to 0.75
- near_list: int32 [2048, 5], P(('oct', 'leaf')), may hold values from 0 to 2047, as said below
- near_count: int32 [2048], P(('oct', 'leaf')), may hold values from 2 to 5, as said below
- leaf_far: int32 [2048, 4], P(('oct', 'leaf')), may hold values from 0 to 2047, as said below
- dev_far: int32 [256, 4], P(('oct', 'leaf')), may hold values from 0 to 255, as said below
- oct_far: int32 [8, 2], P('oct'), may hold values from 0 to 7, as said below
- leaf_skel: int32 [2048, 64], P(('oct', 'leaf')), may hold values from 0 to 511, as said below
- dev_skel: int32 [256, 64], P(('oct', 'leaf')), may hold values from 0 to 511, as said below
- oct_skel: int32 [8, 64], replicated, may hold values from 0 to 2047, as said below
Outputs:
- kernel_product: float32 [64, 1048576], P(None, ('oct', 'leaf'))
- derivative_product: float32 [64, 1048576], P(None, ('oct', 'leaf'))
Inputs may be any that keep to these rules, and one draw needn't show every extreme that they name: `near_list`: slot 0 of a leaf's list is the leaf itself; every entry is a leaf at most 2 places away in Morton order. `near_count`: whole devices are busy: on some devices every leaf uses all 5 slots, elsewhere two to 4. `leaf_far`: every entry is a leaf 3 to 8 places away in Morton order. `dev_far`: every entry is another device node of the same region, distinct within a row. `oct_far`: entries are other regions, distinct within a row. `leaf_skel`: distinct within a row. `dev_skel`: distinct within a row. `oct_skel`: distinct within a row.
All inputs are finite; a program needn't handle non-finite values.
Results may differ from a plain program's by a relative error of at most 0.003.
Values may be sent and summed in bfloat16 or wider, within the bound.
A program may use at most 128 MiB of HBM per device.

v0:
```python
import math

import jax
import jax.numpy as jnp
from jax import lax
from jax.sharding import PartitionSpec as P

LEAF = 512
NEAR_WIN = 2


broad_scale = 6.0
sharp_scale = 0.25
broad_var = 0.08
sharp_var = 0.1
broad_rate = math.sqrt(3.0) / broad_scale
sharp_rate = math.sqrt(3.0) / sharp_scale
highest = lax.Precision.HIGHEST


def with_halo(cells, sides, width):
    for axis, dim in sides:
        count = lax.axis_size(axis)
        ends = count - 1
        head = lax.slice_in_dim(cells, 0, width, axis=dim)
        tail = lax.slice_in_dim(cells, cells.shape[dim] - width, cells.shape[dim], axis=dim)
        cells = jnp.concatenate(
            [
                lax.ppermute(tail, axis, [(i, (i + 1) % count) for i in range(ends)]),
                cells,
                lax.ppermute(head, axis, [((i + 1) % count, i) for i in range(ends)]),
            ],
            axis=dim,
        )
    return cells


def box_anchor(leaf_index):
    corners = []
    for coord_axis in range(3):
        summed = jnp.zeros(leaf_index.shape, jnp.int32)
        for bit_index in range(10):
            summed = summed + (leaf_index >> 3 * bit_index + coord_axis & 1) * (1 << bit_index)
        corners.append(summed)
    return jnp.stack(corners).astype(jnp.float32)


def matern_pair(target, source):
    squared = jnp.zeros((target.shape[1], source.shape[1]), jnp.float32)
    for coord_axis in range(3):
        between = target[coord_axis][:, None] - source[coord_axis][None, :]
        squared = squared + between * between
    distance = jnp.sqrt(squared)
    wide_scaled = broad_rate * distance
    narrow_scaled = sharp_rate * distance
    wide_fading = jnp.exp(-wide_scaled)
    narrow_fading = jnp.exp(-narrow_scaled)
    kernel_value = (
        broad_var * (1.0 + wide_scaled) * wide_fading
        + sharp_var * (1.0 + narrow_scaled) * narrow_fading
    )
    kernel_slope = (
        broad_var * wide_scaled * wide_scaled * wide_fading
        + sharp_var * narrow_scaled * narrow_scaled * narrow_fading
    )
    return (kernel_value, kernel_slope)


def couple(target, source, charges):
    kernel_value, kernel_slope = matern_pair(target, source)
    return jnp.stack(
        [
            jnp.dot(kernel_value, charges, precision=highest),
            jnp.dot(kernel_slope, charges, precision=highest),
        ]
    )


def sum_couple(target, sources, charges):
    return jnp.sum(jax.vmap(couple, (None, 0, 0))(target, sources, charges), axis=0)


def near_term(target_pos, source_pos, source_probes):
    kernel_value, kernel_slope = matern_pair(source_pos, target_pos)
    first = jnp.dot(
        source_probes, kernel_value.astype(jnp.bfloat16), preferred_element_type=jnp.float32
    )
    second = jnp.dot(
        source_probes, kernel_slope.astype(jnp.bfloat16), preferred_element_type=jnp.float32
    )
    return jnp.stack([first, second])


def skipped(target_pos, source_pos, source_probes):
    return jnp.zeros((2, source_probes.shape[0], target_pos.shape[1]), jnp.float32)


def body(
    probes,
    offsets,
    leaf_basis,
    dev_transfer,
    oct_transfer,
    near_list,
    near_count,
    leaf_far,
    dev_far,
    oct_far,
    leaf_skel,
    dev_skel,
    oct_skel,
):
    leaves = near_list.shape[0]
    points = probes.shape[1]
    probe_rows = probes.shape[0]
    skel_rows = leaf_skel.shape[1]
    leaf_count = lax.axis_size("leaf")
    my_oct = lax.axis_index("oct")
    first_leaf = lax.axis_index(("oct", "leaf")) * leaves
    own_leaves = first_leaf + jnp.arange(leaves, dtype=jnp.int32)
    positions = box_anchor(own_leaves)[:, :, None] + offsets.reshape(3, leaves, LEAF).astype(
        jnp.float32
    )
    leaf_pos = jnp.take_along_axis(positions, leaf_skel[None], axis=2)
    leaf_pos_t = jnp.transpose(leaf_pos, (1, 0, 2))
    dev_pos = leaf_pos.reshape(3, leaves * skel_rows)[:, dev_skel[0]]
    halo_width = NEAR_WIN * LEAF
    wide_probes, wide_offsets = (
        with_halo(probes, ((("oct", "leaf"), 1),), halo_width),
        with_halo(offsets, ((("oct", "leaf"), 1),), halo_width),
    )
    wide_leaves = leaves + 2 * NEAR_WIN
    wide_index = jnp.maximum(first_leaf - NEAR_WIN + jnp.arange(wide_leaves, dtype=jnp.int32), 0)
    wide_pos = box_anchor(wide_index)[:, :, None] + wide_offsets.reshape(
        3, wide_leaves, LEAF
    ).astype(jnp.float32)
    leaf_bases = leaf_basis.reshape(leaves, skel_rows, LEAF)
    q_leaf = jnp.einsum(
        "lsn,pln->lsp",
        leaf_bases,
        probes.reshape(probe_rows, leaves, LEAF),
        preferred_element_type=jnp.float32,
    )
    q_dev = jnp.dot(dev_transfer, q_leaf.reshape(leaves * skel_rows, probe_rows), precision=highest)
    upward = jnp.dot(oct_transfer, q_dev, precision=highest)
    wide_q, wide_sk = (
        with_halo(q_leaf, ((("oct", "leaf"), 0),), leaves),
        with_halo(leaf_pos_t, ((("oct", "leaf"), 0),), leaves),
    )
    row_q, row_sk = (
        lax.all_gather(q_dev[None], "leaf", axis=0, tiled=True),
        lax.all_gather(dev_pos[None], "leaf", axis=0, tiled=True),
    )
    oct_q = lax.psum(upward, "leaf")
    row_flat = jnp.transpose(row_sk, (1, 0, 2)).reshape(3, leaf_count * skel_rows)
    oct_pos = row_flat[:, oct_skel[my_oct]]
    every_q, every_sk = (
        lax.all_gather(oct_q[None], "oct", axis=0, tiled=True),
        lax.all_gather(oct_pos[None], "oct", axis=0, tiled=True),
    )
    far_oct = sum_couple(every_sk[my_oct], every_sk[oct_far[0]], every_q[oct_far[0]])
    dev_partner = dev_far[0] % leaf_count
    far_dev = sum_couple(dev_pos, row_sk[dev_partner], row_q[dev_partner])
    down_dev = jnp.einsum("st,ksp->ktp", oct_transfer, far_oct, precision=highest) + far_dev
    leaf_partner = leaf_far - first_leaf + leaves
    far_leaf = jax.vmap(sum_couple)(leaf_pos_t, wide_sk[leaf_partner], wide_q[leaf_partner])
    down_cat = jnp.einsum("sm,ksp->kmp", dev_transfer, down_dev, precision=highest)
    down_leaf = (
        down_cat.reshape(2, leaves, skel_rows, probe_rows) + jnp.transpose(far_leaf, (1, 0, 2, 3))
    ).astype(jnp.bfloat16)
    far_out = jnp.einsum(
        "klsp,lsn->kpln", down_leaf, leaf_bases, preferred_element_type=jnp.float32
    ).reshape(2, probe_rows, points)

    def near_leaf(leaf_slot, totals):
        target_pos = lax.dynamic_index_in_dim(positions, leaf_slot, 1, keepdims=False)
        summed = jnp.zeros((2, probe_rows, LEAF), jnp.float32)
        for slot_index in range(near_list.shape[1]):
            source = near_list[leaf_slot, slot_index] - first_leaf + NEAR_WIN
            source_pos = lax.dynamic_index_in_dim(wide_pos, source, 1, keepdims=False)
            source_probes = lax.dynamic_slice_in_dim(wide_probes, source * LEAF, LEAF, 1)
            summed = summed + lax.cond(
                slot_index < near_count[leaf_slot],
                near_term,
                skipped,
                target_pos,
                source_pos,
                source_probes,
            )
        return lax.dynamic_update_slice_in_dim(totals, summed, leaf_slot * LEAF, 2)

    near_out = lax.fori_loop(0, leaves, near_leaf, jnp.zeros((2, probe_rows, points), jnp.float32))
    result = near_out + far_out
    return (result[0], result[1])


def solution(mesh):
    return jax.shard_map(
        body,
        mesh=mesh,
        in_specs=(
            P(None, ("oct", "leaf")),
            P(None, ("oct", "leaf")),
            P(("oct", "leaf"), None),
            P(("oct", "leaf"), None),
            P(("oct", "leaf"), None),
            P(("oct", "leaf"), None),
            P(("oct", "leaf")),
            P(("oct", "leaf"), None),
            P(("oct", "leaf"), None),
            P("oct", None),
            P(("oct", "leaf"), None),
            P(("oct", "leaf"), None),
            P(),
        ),
        out_specs=(P(None, ("oct", "leaf")), P(None, ("oct", "leaf"))),
        check_vma=False,
    )
```

profile of v0, /device:TPU:8, one launch (start us, length us, event | category | flops | bytes accessed | tf_op | source)
XLA Modules:
  0.0 576.9 jit_solution(3865604887475402025)
XLA Ops:
  3.0 9.3 %collective-permute-start.7 = (f32[8,64,64]{2,1,0:T(8,128)S(1)}, f32[8,64,64]{2,1,0:T(8,128)}, u32[]{:S(2)}, u32[]{:S(2)}) collective-permute-start(f32[8,64,64]{2,1,0:T(8,128)S(1)} %fusion.189), channel_id=1, source_target_pairs={{1,0},{2,1},{3,2},{4,3},{5,4},{6,5},{7,6},{8,7},{9,8},{10,9},{11,1... | collective-permute-start | bytes 393224 | tf_op jit(solution)/shard_map/ppermute | solution.py:31
  12.3 1.9 collective-permute-start.6
  17.5 7.9 %collective-permute-start.3 = (bf16[3,1024]{1,0:T(4,128)(2,1)}, bf16[3,1024]{1,0:T(4,128)(2,1)}, u32[]{:S(2)}, u32[]{:S(2)}) collective-permute-start(bf16[3,1024]{1,0:T(4,128)(2,1)} %get-tuple-element.996), channel_id=1, source_target_pairs={{1,0},{2,1},{3,2},{4,3},{5,4},{6,5},{7,6},{8,7},{9,8},{10,9},{11,1... | collective-permute-start | bytes 18440 | tf_op jit(solution)/shard_map/ppermute | solution.py:31
  26.8 2.5 copy.47
  31.3 6.1 %gather_fusion.8 = f32[512,3]{1,0:T(8,128)} fusion(f32[3,8,512]{0,2,1:T(8,128)S(1)} %broadcast_add_fusion, s32[512]{0:T(512)S(1)} %reshape.1127), kind=kCustom, calls=%fused_computation.8 | custom fusion | bytes 16384 | tf_op jit(solution)/shard_map/jit(take_along_axis)/gather | solution.py:124
  40.4 3.4 collective-permute-start.5
  50.4 51.9 %all-gather.2 = f32[2048,64]{1,0:T(8,128)} all-gather(f32[64,64]{1,0:T(8,128)S(1)} %copy.57), channel_id=4, replica_groups=mesh['oct'=8,'leaf'=32] {'leaf'}, dimensions={0}, use_global_device_ids=true | all-gather | bytes 540672 | tf_op jit(solution)/shard_map/all_gather | solution.py:151
  107.5 47.9 %all-gather.3 = f32[32,3,64]{2,1,0:T(4,128)S(1)} all-gather(f32[1,3,64]{2,1,0:T(4,128)S(1)} %copy.51), channel_id=2, replica_groups=mesh['oct'=8,'leaf'=32] {'leaf'}, dimensions={0}, use_global_device_ids=true | all-gather | bytes 25344 | tf_op jit(solution)/shard_map/all_gather | solution.py:152
  155.4 2.5 gather_fusion.5
  158.5 2.0 convolution_bitcast_fusion.15
  160.5 2.1 convolution_bitcast_fusion.14
  166.1 140.3 %psum.7 = f32[1,64,64]{1,2,0:T(8,128)} all-reduce(f32[1,64,64]{1,2,0:T(8,128)} %convolution_bitcast_fusion.19), channel_id=1, replica_groups=mesh['oct'=8,'leaf'=32] {'leaf'}, use_global_device_ids=true, to_apply=%region_12.13 | all-reduce | flops 4096 | bytes 32768 | tf_op jit(solution)/shard_map/psum | solution.py:154
  307.8 14.7 %all_gather.14 = f32[8,64,64]{2,1,0:T(8,128)} all-gather(f32[1,64,64]{2,1,0:T(8,128)} %copy.55), channel_id=1, replica_groups=mesh['oct'=8,'leaf'=32] {'oct'}, dimensions={0}, use_global_device_ids=true | all-gather | bytes 147456 | tf_op jit(solution)/shard_map/all_gather | solution.py:158
  322.5 2.2 copy.52
  324.8 2.4 gather_fusion.1
  328.6 11.7 %all-gather.4 = f32[8,3,64]{2,1,0:T(4,128)S(1)} all-gather(f32[1,3,64]{2,1,0:T(4,128)} %copy.53), channel_id=3, replica_groups=mesh['oct'=8,'leaf'=32] {'oct'}, dimensions={0}, use_global_device_ids=true | all-gather | bytes 6912 | tf_op jit(solution)/shard_map/all_gather | solution.py:159
  342.1 2.3 gather_fusion.3
  359.2 1.9 collective-permute-start.4
  361.2 1.9 collective-permute-start
  364.0 8.0 %collective-permute-start.1 = (bf16[64,1024]{1,0:T(8,128)(2,1)}, bf16[64,1024]{1,0:T(8,128)(2,1)S(1)}, u32[]{:S(2)}, u32[]{:S(2)}) collective-permute-start(bf16[64,1024]{1,0:T(8,128)(2,1)} %get-tuple-element.991), channel_id=1, source_target_pairs={{1,0},{2,1},{3,2},{4,3},{5,4},{6,5},{7,6},{8,7},{9,8},{10,9},{11,1... | collective-permute-start | bytes 393224 | tf_op jit(solution)/shard_map/ppermute | solution.py:31
  376.2 3.5 convolution_bitcast_fusion.12
  379.8 2.3 convolution_bitcast_fusion.11
  385.9 187.1 %while.16 = (s32[]{:T(128)}, f32[2,64,4096]{2,1,0:T(8,128)}, s32[8]{0:T(128)S(1)}, f32[3,8,512]{2,0,1:T(4,128)S(1)}, s32[8,5]{1,0:T(8,128)S(1)}, /*index=5*/s32[...) while((s32[]{:T(128)}, f32[2,64,4096]{2,1,0:T(8,128)}, ...), condition=%wide.region_11.12_spmd, body=%wide.region_0.11_spmd.sunk | while | flops 388563008 | bytes 6419621 | solution.py:192
  389.3 3.9 conditional.14
  393.2 3.7 conditional.13
  396.9 3.9 conditional.12
  400.9 3.9 conditional.11
  404.8 3.7 conditional.10
  412.7 3.9 conditional.14
  416.6 3.7 conditional.13
  420.3 3.9 conditional.12
  424.2 3.9 conditional.11
  428.1 3.7 conditional.10
  436.1 3.9 conditional.14
  440.0 3.7 conditional.13
  443.7 3.9 conditional.12
  447.6 3.9 conditional.11
  451.5 3.7 conditional.10
  459.5 3.9 conditional.14
  463.4 3.7 conditional.13
  467.1 3.9 conditional.12
  471.0 3.9 conditional.11
  474.9 3.7 conditional.10
  482.9 3.9 conditional.14
  486.8 3.7 conditional.13
  490.5 3.9 conditional.12
  494.4 3.9 conditional.11
  498.3 3.7 conditional.10
  506.3 3.9 conditional.14
  510.1 3.7 conditional.13
  513.8 3.9 conditional.12
  517.8 3.9 conditional.11
  521.7 3.7 conditional.10
  529.6 3.9 conditional.14
  533.5 3.7 conditional.13
  537.2 3.9 conditional.12
  541.1 3.9 conditional.11
  545.0 3.7 conditional.10
  553.0 3.9 conditional.14
  556.9 3.7 conditional.13
  560.6 3.9 conditional.12
  564.5 3.9 conditional.11
  568.4 3.7 conditional.10
  573.0 2.5 add.1482
  (369 shorter events, 195.2 us)
Async XLA Ops:
  0.6 1.0 copy-start
  3.0 370.5 %collective-permute-start.7 = (f32[8,64,64]{2,1,0:T(8,128)S(1)}, f32[8,64,64]{2,1,0:T(8,128)}, u32[]{:S(2)}, u32[]{:S(2)}) collective-permute-start(f32[8,64,64]{2,1,0:T(8,128)S(1)} %fusion.189), channel_id=1, source_target_pairs={{1,0},{2,1},{3,2},{4,3},{5,4},{6,5},{7,6},{8,7},{9,8},{10,9},{11,1... | collective-permute-start | bytes 393224 | tf_op jit(solution)/shard_map/ppermute | solution.py:31
  12.3 361.2 %collective-permute-start.6 = (f32[8,64,64]{2,1,0:T(8,128)S(1)}, f32[8,64,64]{2,1,0:T(8,128)}, u32[]{:S(2)}, u32[]{:S(2)}) collective-permute-start(f32[8,64,64]{2,1,0:T(8,128)S(1)} %fusion.189), channel_id=1, source_target_pairs={{0,1},{1,2},{2,3},{3,4},{4,5},{5,6},{6,7},{7,8},{8,9},{9,10},{10,1... | collective-permute-start | bytes 393224 | tf_op jit(solution)/shard_map/ppermute | solution.py:29
  15.6 343.7 %collective-permute-start.2 = (bf16[3,1024]{1,0:T(4,128)(2,1)}, bf16[3,1024]{1,0:T(4,128)(2,1)}, u32[]{:S(2)}, u32[]{:S(2)}) collective-permute-start(bf16[3,1024]{1,0:T(4,128)(2,1)} %get-tuple-element.995), channel_id=1, source_target_pairs={{0,1},{1,2},{2,3},{3,4},{4,5},{5,6},{6,7},{7,8},{8,9},{9,10},{10,1... | collective-permute-start | bytes 18440 | tf_op jit(solution)/shard_map/ppermute | solution.py:29
  17.5 343.7 %collective-permute-start.3 = (bf16[3,1024]{1,0:T(4,128)(2,1)}, bf16[3,1024]{1,0:T(4,128)(2,1)}, u32[]{:S(2)}, u32[]{:S(2)}) collective-permute-start(bf16[3,1024]{1,0:T(4,128)(2,1)} %get-tuple-element.996), channel_id=1, source_target_pairs={{1,0},{2,1},{3,2},{4,3},{5,4},{6,5},{7,6},{8,7},{9,8},{10,9},{11,1... | collective-permute-start | bytes 18440 | tf_op jit(solution)/shard_map/ppermute | solution.py:31
  29.4 15.5 %copy-start.1 = (bf16[64,4096]{1,0:T(8,128)(2,1)S(1)}, bf16[64,4096]{1,0:T(8,128)(2,1)}, u32[]{:S(2)}) copy-start(bf16[64,4096]{1,0:T(8,128)(2,1)} %param.25) | copy-start | bytes 1572868
  29.5 19.0 %copy-start.3 = (f32[64,512]{1,0:T(8,128)S(1)}, f32[64,512]{1,0:T(8,128)}, u32[]{:S(2)}) copy-start(f32[64,512]{1,0:T(8,128)} %param.28) | copy-start | bytes 393220
  40.4 323.7 %collective-permute-start.5 = (f32[8,3,64]{2,1,0:T(4,128)}, f32[8,3,64]{2,1,0:T(4,128)}, u32[]{:S(2)}, u32[]{:S(2)}) collective-permute-start(f32[8,3,64]{2,1,0:T(4,128)} %select_bitcast_fusion), channel_id=1, source_target_pairs={{1,0},{2,1},{3,2},{4,3},{5,4},{6,5},{7,6},{8,7},{9,8},{10,9},{11,1... | collective-permute-start | bytes 18440 | tf_op jit(solution)/shard_map/ppermute | solution.py:31
  155.4 3.0 copy-start.5
  160.5 195.2 %copy-start.4 = (f32[64,512]{1,0:T(8,128)S(1)}, f32[64,512]{1,0:T(8,128)}, u32[]{:S(2)}) copy-start(f32[64,512]{1,0:T(8,128)} %param.28) | copy-start | bytes 393220
  342.1 14.6 %copy-start.10 = (s32[1,12]{1,0:T(1,128)S(1)}, s32[1,12]{1,0:T(1,128)}, u32[]{:S(2)}) copy-start(s32[1,12]{1,0:T(1,128)} %multiply_add_fusion.5) | copy-start | bytes 148
  342.1 14.6 %copy-start.11 = (s32[1,12]{1,0:T(1,128)S(1)}, s32[1,12]{1,0:T(1,128)}, u32[]{:S(2)}) copy-start(s32[1,12]{1,0:T(1,128)} %get-tuple-element.1009) | copy-start | bytes 148
  356.7 6.4 %copy-start.6 = (bf16[3,4096]{1,0:T(4,128)(2,1)S(1)}, bf16[3,4096]{1,0:T(4,128)(2,1)}, u32[]{:S(2)}) copy-start(bf16[3,4096]{1,0:T(4,128)(2,1)} %param.26) | copy-start | bytes 73732
  359.2 12.8 %collective-permute-start.4 = (f32[8,3,64]{2,1,0:T(4,128)}, f32[8,3,64]{2,1,0:T(4,128)S(1)}, u32[]{:S(2)}, u32[]{:S(2)}) collective-permute-start(f32[8,3,64]{2,1,0:T(4,128)} %select_bitcast_fusion), channel_id=1, source_target_pairs={{0,1},{1,2},{2,3},{3,4},{4,5},{5,6},{6,7},{7,8},{8,9},{9,10},{10,1... | collective-permute-start | bytes 18440 | tf_op jit(solution)/shard_map/ppermute | solution.py:29
  361.2 23.2 %collective-permute-start = (bf16[64,1024]{1,0:T(8,128)(2,1)}, bf16[64,1024]{1,0:T(8,128)(2,1)S(1)}, u32[]{:S(2)}, u32[]{:S(2)}) collective-permute-start(bf16[64,1024]{1,0:T(8,128)(2,1)} %get-tuple-element.990), channel_id=1, source_target_pairs={{0,1},{1,2},{2,3},{3,4},{4,5},{5,6},{6,7},{7,8},{8,9},{9,10},{10,1... | collective-permute-start | bytes 393224 | tf_op jit(solution)/shard_map/ppermute | solution.py:29
  363.9 12.3 %copy-start.7 = (f32[8,1,64]{2,1,0:T(1,128)S(1)}, f32[8,1,64]{2,1,0:T(1,128)}, u32[]{:S(2)}) copy-start(f32[8,1,64]{2,1,0:T(1,128)} %get-tuple-element.997) | copy-start | bytes 6148
  363.9 12.3 %copy-start.8 = (f32[8,1,64]{2,1,0:T(1,128)S(1)}, f32[8,1,64]{2,1,0:T(1,128)}, u32[]{:S(2)}) copy-start(f32[8,1,64]{2,1,0:T(1,128)} %get-tuple-element.998) | copy-start | bytes 6148
  363.9 12.3 %copy-start.9 = (f32[8,1,64]{2,1,0:T(1,128)S(1)}, f32[8,1,64]{2,1,0:T(1,128)}, u32[]{:S(2)}) copy-start(f32[8,1,64]{2,1,0:T(1,128)} %get-tuple-element.999) | copy-start | bytes 6148
  364.0 20.3 %collective-permute-start.1 = (bf16[64,1024]{1,0:T(8,128)(2,1)}, bf16[64,1024]{1,0:T(8,128)(2,1)S(1)}, u32[]{:S(2)}, u32[]{:S(2)}) collective-permute-start(bf16[64,1024]{1,0:T(8,128)(2,1)} %get-tuple-element.991), channel_id=1, source_target_pairs={{1,0},{2,1},{3,2},{4,3},{5,4},{6,5},{7,6},{8,7},{9,8},{10,9},{11,1... | collective-permute-start | bytes 393224 | tf_op jit(solution)/shard_map/ppermute | solution.py:31
  376.2 3.6 copy-start.2
  384.3 1.6 copy-start.12
  384.3 1.6 copy-start.13
where the time goes:
time: 580 us; the launch traced here: 577 us
  blocking collectives  267 us (46%)
  matrix products  120 us (21%)
  local copies, waits for them, and re-layouts  75.5 us (13%)
  loops' own time  49.7 us (9%)
  starting transfers between devices  36.2 us (6%)
  other arithmetic  27.7 us (5%)
    psum x1, blocking collectives, body(): oct_q = lax.psum(upward, 'leaf')  140 us
    all_gather x1, blocking collectives, body(): lax.all_gather(q_dev[None], 'leaf', axis=0, tiled=True)  51.9 us
    dot_general x40, matrix products, near_term(): jnp.dot(source_probes, kernel_slope.astype(jnp.bfloat16), preferred_eleme...  50.1 us
    dot_general x40, matrix products, near_term(): jnp.dot(source_probes, kernel_value.astype(jnp.bfloat16), preferred_eleme...  50 us
    all_gather x1, blocking collectives, body(): lax.all_gather(dev_pos[None], 'leaf', axis=0, tiled=True)  47.9 us
    ppermute x4, starting transfers between devices, with_halo(): lax.ppermute(head, axis, [((i + 1) % count, i) for i in range(ends)])  28.5 us
    another operation x40, loops' own time, near_leaf(): lax.cond(slot_index < near_count[leaf_slot], near_term, skipped, target_p...  26.9 us
    dynamic_slice x40, local copies, waits for them, and re-layouts, near_leaf(): source = near_list[leaf_slot, slot_index] - first_leaf + NEAR_WIN  24.2 us
  transfers between devices with their start and end apart: 8, of which 0 were waited for; matrix products, arithmetic and copies ran while one was open for 14% of the time, Pallas kernels for 0%

commit v1 on v0

v1 whole, which is shorter than its diff:
```python
import functools
import math

import jax
import jax.numpy as jnp
from jax import lax
from jax.experimental import pallas as pl
from jax.experimental.pallas import tpu as pltpu
from jax.sharding import PartitionSpec as P

LEAF = 512
SKEL = 64
PROBES = 64
LEAVES = 8
WIN = 2
EXT = LEAVES + 2 * WIN
WIDE = 3 * LEAVES
RED = 9
FEAT = 64

MESH = pl.DeviceIdType.MESH
f32 = jnp.float32
bf16 = jnp.bfloat16
LOG2E = math.log2(math.e)
NN = (((1,), (0,)), ((), ()))
NT = (((1,), (1,)), ((), ()))


def dot(a, b, dims=NN):
    return lax.dot_general(a, b, dims, preferred_element_type=f32)


def halves(v):
    high = v.astype(bf16)
    return high, (v - high.astype(f32)).astype(bf16)


def dot3(a, b, dims=NN):
    ah, al = halves(a)
    bh, bl = halves(b)
    return dot(ah, bh, dims) + (dot(ah, bl, dims) + dot(al, bh, dims))


def split3(v):
    high = v.astype(bf16).astype(f32)
    rest = v - high
    mid = rest.astype(bf16).astype(f32)
    return high, mid, (rest - mid).astype(bf16).astype(f32)


def matern(w):
    w = jnp.maximum(w, 1e-30)
    t = w * lax.rsqrt(w)
    wide = jnp.exp2(t * (-LOG2E))
    cube = wide * wide * wide
    six = cube * cube
    twelve = six * six
    sharp = twelve * twelve
    wide = 0.08 * wide
    value = (wide + 0.1 * sharp) + t * (wide + 2.4 * sharp)
    slope = w * (wide + 57.6 * sharp)
    return value, slope


def box_corner(leaf):
    corner = []
    for axis in range(3):
        total = 0
        for bit in range(4):
            total = total + ((leaf >> (3 * bit + axis)) & 1) * (1 << bit)
        corner.append(total)
    return corner


def rows_of(corner, shape):
    row = lax.broadcasted_iota(jnp.int32, shape, 0)
    x, y, z = [jnp.asarray(c, jnp.int32).astype(f32) for c in corner]
    return jnp.where(row == 0, x, jnp.where(row == 1, y, jnp.where(row == 2, z, 0.0)))


def inside(index, count):
    return jnp.minimum(jnp.maximum(index, 0), count - 1)


def stacked(v):
    return jnp.concatenate([v[:, :SKEL], v[:, SKEL:]], axis=0)


def far_tile(columns, source):
    w = None
    for axis in range(3):
        gap = columns[axis] - source[axis : axis + 1, :]
        w = gap * gap if w is None else w + gap * gap
    value, slope = matern(w * (1.0 / 12.0))
    return jnp.concatenate([value, slope], axis=0)


def kernel(
    n_oct,
    n_leaf,
    probes,
    offsets,
    basis,
    dev_transfer,
    oct_transfer,
    leaf_skel,
    dev_skel,
    oct_skel,
    near_list,
    near_count,
    leaf_far,
    dev_far,
    oct_far,
    out_value,
    out_slope,
    pext,
    oext,
    wq,
    wsk,
    ag,
    tiles,
    gathered,
    regions,
    chosen,
    spread,
    feat_f,
    feat_g,
    kv0,
    ks0,
    kv1,
    ks1,
    acc,
    columns,
    far_sum,
    halo_send,
    halo_recv,
    ag_send,
    ag_recv,
    red_send,
    red_recv,
    oct_send,
    oct_recv,
    spread_send,
    spread_recv,
):
    o = lax.axis_index("oct")
    me = lax.axis_index("leaf")
    flat = o * n_leaf + me
    devices = n_oct * n_leaf
    right = lax.rem(flat + 1, devices)
    left = lax.rem(flat + devices - 1, devices)
    right_id = (right // n_leaf, lax.rem(right, n_leaf))
    left_id = (left // n_leaf, lax.rem(left, n_leaf))
    first = flat * LEAVES

    def in_region(k):
        return lax.rem(me + k, n_leaf)

    def across(k):
        return lax.rem(o + k, n_oct)

    barrier = pltpu.get_barrier_semaphore()

    def greet(device):
        pl.semaphore_signal(barrier, inc=1, device_id=device, device_id_type=MESH)

    greet(right_id)
    greet(left_id)

    def greet_region(k, _):
        greet((o, in_region(k)))
        return 0

    lax.fori_loop(1, n_leaf, greet_region, 0)

    def greet_across(k, _):
        greet((across(k), me))
        return 0

    lax.fori_loop(1, n_oct, greet_across, 0)

    base = box_corner(first)
    row512 = lax.broadcasted_iota(jnp.int32, (LEAF, SKEL), 0)
    charges, picked, corners = [], [], []
    for leaf in range(LEAVES):
        span = slice(leaf * LEAF, (leaf + 1) * LEAF)
        pext[WIN + leaf] = probes[:, span]
        own = jnp.concatenate([offsets[:, span].astype(f32), jnp.zeros((5, LEAF), f32)], axis=0)
        oext[WIN + leaf] = own
        one_hot = jnp.where(row512 == leaf_skel[leaf : leaf + 1, :], 1.0, 0.0).astype(bf16)
        picked.append(dot(own.astype(bf16), one_hot))
        corner = [base[0] + (leaf & 1), base[1] + (leaf >> 1 & 1), base[2] + (leaf >> 2 & 1)]
        corners.append(rows_of(corner, (8, SKEL)))
        wsk[LEAVES + leaf] = picked[-1] + corners[-1]
        charge = dot(pext[WIN + leaf], basis[leaf * SKEL : (leaf + 1) * SKEL, :], NT)
        charges.append(charge)
        wq[LEAVES + leaf] = jnp.concatenate(halves(charge), axis=1)
    q_dev = dot3(jnp.concatenate(charges, axis=1), dev_transfer[...], NT)
    upward = dot3(q_dev, oct_transfer[...], NT)
    both = jnp.concatenate(
        [jnp.concatenate(picked, axis=1), jnp.concatenate(corners, axis=1)], axis=0
    ).astype(bf16)
    one_hot = jnp.where(row512 == dev_skel[...], 1.0, 0.0).astype(bf16)
    dev_both = dot(both, one_hot)
    dev_pos = dev_both[:8] + dev_both[8:]
    ag[me] = jnp.concatenate(
        [q_dev, jnp.concatenate([dev_both, jnp.zeros((PROBES - 16, SKEL), f32)], axis=0)], axis=1
    ).astype(bf16)
    wanted = oct_skel[pl.ds(o, 1), :] - me * SKEL
    row64 = lax.broadcasted_iota(jnp.int32, (SKEL, SKEL), 0)
    one_hot = jnp.where(row64 == wanted, 1.0, 0.0).astype(bf16)
    oct_both = dot(dev_both.astype(bf16), one_hot)
    blank = jnp.zeros((8, SKEL), f32)
    for t in range(RED - 1):
        tiles[t] = jnp.concatenate([upward[8 * t : 8 * t + 8], blank], axis=1)
    tiles[RED - 1] = jnp.concatenate([oct_both[:8] + oct_both[8:], blank], axis=1)

    pl.semaphore_wait(barrier, n_leaf - 1 + n_oct - 1 + 2)

    def copy(src, dst, send, recv, device):
        return pltpu.make_async_remote_copy(
            src_ref=src,
            dst_ref=dst,
            send_sem=send,
            recv_sem=recv,
            device_id=device,
            device_id_type=MESH,
        )

    def reduce_copy(t, slot):
        return copy(
            tiles.at[t], gathered.at[slot], red_send.at[t], red_recv.at[slot], (o, t)
        )

    for t in range(RED):

        @pl.when(me != t)
        def _():
            reduce_copy(t, me).start()

    @pl.when(me < RED)
    def _():
        gathered[me] = tiles[me]

    own = slice(LEAVES, 2 * LEAVES)
    halo = [
        copy(pext.at[WIN : 2 * WIN], pext.at[WIN + LEAVES : EXT], halo_send.at[0], halo_recv.at[0], left_id),
        copy(oext.at[WIN : 2 * WIN], oext.at[WIN + LEAVES : EXT], halo_send.at[1], halo_recv.at[1], left_id),
        copy(pext.at[LEAVES : LEAVES + WIN], pext.at[0:WIN], halo_send.at[2], halo_recv.at[2], right_id),
        copy(oext.at[LEAVES : LEAVES + WIN], oext.at[0:WIN], halo_send.at[3], halo_recv.at[3], right_id),
        copy(wq.at[own], wq.at[2 * LEAVES : WIDE], halo_send.at[4], halo_recv.at[4], left_id),
        copy(wsk.at[own], wsk.at[2 * LEAVES : WIDE], halo_send.at[5], halo_recv.at[5], left_id),
        copy(wq.at[own], wq.at[0:LEAVES], halo_send.at[6], halo_recv.at[6], right_id),
        copy(wsk.at[own], wsk.at[0:LEAVES], halo_send.at[7], halo_recv.at[7], right_id),
    ]
    for piece in halo:
        piece.start()

    def gather_copy(peer, slot):
        return copy(ag.at[me], ag.at[slot], ag_send.at[peer], ag_recv.at[slot], (o, peer))

    def gather_start(k, _):
        gather_copy(in_region(k), me).start()
        return 0

    lax.fori_loop(1, n_leaf, gather_start, 0)

    row8 = lax.broadcasted_iota(jnp.int32, (8, LEAF), 0)

    def features(e, corner):
        off = oext[e]
        anchor = rows_of(corner, (8, LEAF))
        pos = off + anchor
        norm = split3(jnp.sum(pos * pos, axis=0, keepdims=True) * (1.0 / 12.0))
        parts = split3(pos * (-1.0 / 6.0))

        def mixed(at):
            v = jnp.zeros((8, LEAF), f32)
            for i in range(3):
                v = jnp.where(row8 == at + i, norm[i], v)
            return jnp.where((row8 >= 3 - at) & (row8 < 6 - at), 1.0, v)

        pad = jnp.zeros((8, LEAF), f32)
        rows_f = jnp.concatenate([*parts, *parts, mixed(0), pad], axis=0)
        feat_f[e] = jnp.transpose(rows_f).astype(bf16)
        rows_g = jnp.concatenate([anchor] * 3 + [off] * 3 + [mixed(3), pad], axis=0)
        feat_g[e] = rows_g.astype(bf16)

    for leaf in range(LEAVES):
        features(WIN + leaf, [leaf & 1, leaf >> 1 & 1, leaf >> 2 & 1])
    for e in range(EXT):
        acc[e] = jnp.zeros((2, PROBES, LEAF), f32)

    def uses(target, source):
        leaf = lax.rem(target + LEAVES - WIN, LEAVES)
        wanted_leaf = first + source - WIN
        count = near_count[leaf]
        total = jnp.float32(0.0)
        for s in range(near_list.shape[1]):
            hit = (near_list[leaf, s] == wanted_leaf) & (s < count)
            total = total + jnp.where(hit, jnp.float32(1.0), jnp.float32(0.0))
        return total

    def tile(a, b, kv, ks, rows, cols):
        value, slope = matern(dot(feat_f[a, rows, :], feat_g[b, :, cols]))
        kv[rows, cols] = value.astype(bf16)
        ks[rows, cols] = slope.astype(bf16)

    def interleave(first_ops, second_ops):
        done = 0
        for i, op in enumerate(first_ops):
            op()
            upto = (i + 1) * len(second_ops) // len(first_ops)
            for q in range(done, upto):
                second_ops[q]()
            done = upto

    def pipe(n, make, use, between=lambda k: None):
        bufs = ((kv0, ks0), (kv1, ks1))
        for op in make(0, *bufs[0]):
            op()
        steps = (n - 1) // 2

        def body(k, _):
            between(k)
            interleave(make(2 * k + 1, *bufs[1]), use(2 * k, *bufs[0]))
            interleave(make(2 * k + 2, *bufs[0]), use(2 * k + 1, *bufs[1]))
            return 0

        lax.fori_loop(0, steps, body, 0)
        if n % 2:
            for op in use(n - 1, *bufs[0]):
                op()
        else:
            interleave(make(n - 1, *bufs[1]), use(n - 2, *bufs[0]))
            for op in use(n - 1, *bufs[1]):
                op()

    half = LEAF // 2
    low, high, full = slice(0, half), slice(half, LEAF), slice(0, LEAF)

    def self_make(i, kv, ks):
        e = i + WIN
        ops = []
        for r in range(0, LEAF, 64):
            cols = full if r < half else high
            ops.append(lambda r=r, cols=cols: tile(e, e, kv, ks, slice(r, r + 64), cols))
        return ops

    def self_use(i, kv, ks):
        e = i + WIN
        c = uses(e, e)
        ops = []
        for m, k in enumerate((kv, ks)):

            def upper(m=m, k=k):
                acc[e, m] = c * dot(pext[e, :, low], k[low, :])

            def corner(m=m, k=k):
                acc[e, m, :, high] += c * dot(pext[e, :, high], k[high, high])

            def lower(m=m, k=k):
                acc[e, m, :, low] += c * dot(pext[e, :, high], k[low, high], NT)

            ops += [upper, corner, lower]
        return ops

    pipe(LEAVES, self_make, self_use)

    for piece in halo:
        piece.wait_recv()
    for e in list(range(WIN)) + list(range(WIN + LEAVES, EXT)):
        leaf = lax.rem(first + devices * LEAVES + e - WIN, devices * LEAVES)
        there = box_corner(leaf)
        features(e, [there[i] - base[i] for i in range(3)])

    def pair(i):
        s = (i + 1) // 10
        a = i + 1 - 10 * s
        return a, a + 1 + s

    def pair_make(i, kv, ks):
        a, b = pair(i)
        return [
            lambda r=r: tile(a, b, kv, ks, slice(r, r + 64), full) for r in range(0, LEAF, 64)
        ]

    def pair_use(i, kv, ks):
        a, b = pair(i)
        to_b = uses(b, a)
        to_a = uses(a, b)
        ops = []
        for m, k in enumerate((kv, ks)):
            for span in (low, high):

                def forward(m=m, k=k, span=span):
                    acc[b, m, :, span] += to_b * dot(pext[a], k[:, span])

                def back(m=m, k=k, span=span):
                    acc[a, m, :, span] += to_a * dot(pext[b], k[span, :], NT)

                ops += [forward, back]
        return ops

    def oct_copy(k, slot):
        return copy(
            tiles.at[0], regions.at[slot], oct_send.at[k], oct_recv.at[slot], (across(k), me)
        )

    def spread_copy(peer, slot):
        return copy(chosen, spread.at[slot], spread_send.at[peer], spread_recv.at[slot], (o, peer))

    def each(lo, hi, fn):
        def step(k, _):
            fn(k)
            return 0

        lax.fori_loop(lo, hi, step, 0)

    def sum_region():
        @pl.when(me < RED)
        def _():
            each(1, n_leaf, lambda k: reduce_copy(0, in_region(k)).wait_recv())
            for t in range(RED):

                @pl.when(me != t)
                def _():
                    reduce_copy(t, me).wait_send()

            total = jnp.sum(gathered[...], axis=0)
            regions[o] = total
            tiles[0] = total
            each(1, n_oct, lambda k: oct_copy(k, o).start())

    def spread_regions():
        @pl.when(me < RED)
        def _():
            each(1, n_oct, lambda k: oct_copy(k, across(k)).wait_recv())
            one, two = [regions[inside(oct_far[0, i], n_oct)] for i in range(2)]
            message = [jnp.concatenate([one[:, :SKEL], two[:, :SKEL]], axis=1), regions[o]]
            for m in range(2):
                chosen[m] = message[m]
                spread[me, m] = message[m]
            each(1, n_leaf, lambda k: spread_copy(in_region(k), me).start())

    def between(k):
        pl.when(k == 1)(sum_region)
        pl.when(k == 4)(spread_regions)

    pipe(19, pair_make, pair_use, between)

    upright = jnp.concatenate(
        [wsk[LEAVES + leaf] for leaf in range(LEAVES)] + [dev_pos] + [blank] * 7, axis=0
    )
    upright = jnp.transpose(upright)
    wide = (SKEL, 2 * SKEL)
    for leaf in range(LEAVES + 1):
        for axis in range(3):
            at = 8 * leaf + axis
            columns[leaf, axis] = jnp.broadcast_to(upright[:, at : at + 1], wide)

    def leaf_field(leaf, _):
        targets = [columns[leaf, axis] for axis in range(3)]
        total = jnp.zeros(wide, f32)
        for pairing in range(2):
            x = inside(leaf_far[leaf, 2 * pairing] - first + LEAVES, WIDE)
            y = inside(leaf_far[leaf, 2 * pairing + 1] - first + LEAVES, WIDE)
            source = jnp.concatenate([wsk[x], wsk[y]], axis=1)
            one, two = wq[x], wq[y]
            high = jnp.concatenate([one[:, :SKEL], two[:, :SKEL]], axis=1)
            rest = jnp.concatenate([one[:, SKEL:], two[:, SKEL:]], axis=1)
            tile_high, tile_rest = halves(far_tile(targets, source))
            total += dot(high, tile_high, NT) + (dot(rest, tile_high, NT) + dot(high, tile_rest, NT))
        far_sum[leaf] = total
        return 0

    lax.fori_loop(0, LEAVES, leaf_field, 0)

    each(1, n_leaf, lambda k: gather_copy(me, in_region(k)).wait_recv())
    targets = [columns[LEAVES, axis] for axis in range(3)]
    dev_sum = jnp.zeros(wide, f32)
    for pairing in range(2):
        pieces = [
            ag[inside(dev_far[0, 2 * pairing + i] - o * n_leaf, n_leaf)].astype(f32)
            for i in range(2)
        ]
        source = jnp.concatenate([v[:8, SKEL:] + v[8:16, SKEL:] for v in pieces], axis=1)
        charge = jnp.concatenate([v[:, :SKEL] for v in pieces], axis=1)
        dev_sum += dot3(charge, far_tile(targets, source), NT)

    for t in range(RED):

        @pl.when(me != t)
        def _():
            spread_copy(t, t).wait_recv()

    charge = spread[0 : RED - 1, 0].reshape(PROBES, 2 * SKEL)
    source = spread[RED - 1, 0]
    upright = jnp.transpose(
        jnp.concatenate([spread[RED - 1, 1], jnp.zeros((120, 2 * SKEL), f32)], axis=0)
    )
    targets = [upright[:SKEL, axis : axis + 1] for axis in range(3)]
    oct_sum = dot3(charge, far_tile(targets, source), NT)
    down_dev = dot3(stacked(oct_sum), oct_transfer[...]) + stacked(dev_sum)
    down = dot3(down_dev, dev_transfer[...])
    for leaf in range(LEAVES):
        span = slice(leaf * LEAF, (leaf + 1) * LEAF)
        cols = slice(leaf * SKEL, (leaf + 1) * SKEL)
        mine = (down[:, cols] + stacked(far_sum[leaf])).astype(bf16)
        field = dot(mine, basis[cols, :])
        out_value[:, span] = acc[WIN + leaf, 0] + field[:PROBES]
        out_slope[:, span] = acc[WIN + leaf, 1] + field[PROBES:]

    for piece in halo:
        piece.wait_send()
    each(1, n_leaf, lambda k: gather_copy(in_region(k), me).wait_send())

    @pl.when(me < RED)
    def _():
        each(1, n_oct, lambda k: oct_copy(k, o).wait_send())
        each(1, n_leaf, lambda k: spread_copy(in_region(k), me).wait_send())

    @pl.when(me >= RED)
    def _():
        for t in range(RED):
            reduce_copy(t, me).wait_send()


def body(n_oct, n_leaf, *args):
    (
        probes,
        offsets,
        leaf_basis,
        dev_transfer,
        oct_transfer,
        near_list,
        near_count,
        leaf_far,
        dev_far,
        oct_far,
        leaf_skel,
        dev_skel,
        oct_skel,
    ) = args
    vmem = pl.BlockSpec(memory_space=pltpu.VMEM)
    smem = pl.BlockSpec(memory_space=pltpu.SMEM)
    points = probes.shape[1]
    dma = pltpu.SemaphoreType.DMA
    out = jax.ShapeDtypeStruct((PROBES, points), f32)
    return pl.pallas_call(
        functools.partial(kernel, n_oct, n_leaf),
        out_shape=(out, out),
        in_specs=[vmem] * 8 + [smem] * 5,
        out_specs=(vmem, vmem),
        scratch_shapes=[
            pltpu.VMEM((EXT, PROBES, LEAF), bf16),
            pltpu.VMEM((EXT, 8, LEAF), f32),
            pltpu.VMEM((WIDE, PROBES, 2 * SKEL), bf16),
            pltpu.VMEM((WIDE, 8, SKEL), f32),
            pltpu.VMEM((n_leaf, PROBES, 2 * SKEL), bf16),
            pltpu.VMEM((RED, 8, 2 * SKEL), f32),
            pltpu.VMEM((n_leaf, 8, 2 * SKEL), f32),
            pltpu.VMEM((n_oct, 8, 2 * SKEL), f32),
            pltpu.VMEM((2, 8, 2 * SKEL), f32),
            pltpu.VMEM((RED, 2, 8, 2 * SKEL), f32),
            pltpu.VMEM((EXT, LEAF, FEAT), bf16),
            pltpu.VMEM((EXT, FEAT, LEAF), bf16),
            pltpu.VMEM((LEAF, LEAF), bf16),
            pltpu.VMEM((LEAF, LEAF), bf16),
            pltpu.VMEM((LEAF, LEAF), bf16),
            pltpu.VMEM((LEAF, LEAF), bf16),
            pltpu.VMEM((EXT, 2, PROBES, LEAF), f32),
            pltpu.VMEM((LEAVES + 1, 3, SKEL, 2 * SKEL), f32),
            pltpu.VMEM((LEAVES, PROBES, 2 * SKEL), f32),
            dma((8,)),
            dma((8,)),
            dma((n_leaf,)),
            dma((n_leaf,)),
            dma((RED,)),
            dma((n_leaf,)),
            dma((n_oct,)),
            dma((n_oct,)),
            dma((n_leaf,)),
            dma((n_leaf,)),
        ],
        compiler_params=pltpu.CompilerParams(
            collective_id=0, has_side_effects=True, vmem_limit_bytes=48 * 2**20
        ),
    )(
        probes,
        offsets,
        leaf_basis,
        dev_transfer,
        oct_transfer,
        leaf_skel,
        dev_skel,
        oct_skel,
        near_list,
        near_count,
        leaf_far,
        dev_far,
        oct_far,
    )


def solution(mesh):
    return jax.shard_map(
        functools.partial(body, mesh.shape["oct"], mesh.shape["leaf"]),
        mesh=mesh,
        in_specs=(
            P(None, ("oct", "leaf")),
            P(None, ("oct", "leaf")),
            P(("oct", "leaf"), None),
            P(("oct", "leaf"), None),
            P(("oct", "leaf"), None),
            P(("oct", "leaf"), None),
            P(("oct", "leaf")),
            P(("oct", "leaf"), None),
            P(("oct", "leaf"), None),
            P("oct", None),
            P(("oct", "leaf"), None),
            P(("oct", "leaf"), None),
            P(),
        ),
        out_specs=(P(None, ("oct", "leaf")), P(None, ("oct", "leaf"))),
        check_vma=False,
    )
```

time: 580 us -> 64.6 us (0.11)
  the two profiles are of different devices: /device:TPU:8 before, /device:TPU:1 now
where the time goes in v1:
time: 64.6 us; the launch traced here: 64.2 us
  Pallas kernels  54.8 us (85%)
  local copies, waits for them, and re-layouts  8.62 us (13%)
  between operations  0.71 us (1%)
    pallas_call x1, Pallas kernels, body(): pl.pallas_call(functools.partial(kernel, n_oct, n_leaf), out_shape=(out,...  54.8 us
    unnamed x27, local copies, waits for them, and re-layouts  8.62 us

profile of v1, /device:TPU:1, one launch (start us, length us, event | category | flops | bytes accessed | tf_op | source)
XLA Modules:
  0.0 64.2 jit_solution(18174592261148733359)
XLA Ops:
  0.6 0.0 copy-start.8
  0.6 0.0 copy-start.5
  0.7 0.0 copy-start.11
  0.7 0.0 copy-start.10
  0.7 0.0 copy-start.9
  0.7 0.8 %copy.15.leaf_far = s32[8,4]{1,0:T(8,128)S(1)} copy(s32[8,4]{0,1:T(4,128)} %param.20) | data formatting | bytes 256 | tf_op args[7]
  1.5 0.0 copy-done.8
  1.5 0.0 copy-done.5
  1.5 0.0 copy-done.11
  1.5 0.0 copy-done.10
  1.5 0.0 copy-done.9
  1.5 0.0 copy-start
  1.5 1.0 %copy-done = bf16[64,4096]{1,0:T(8,128)(2,1)S(1)} copy-done((bf16[64,4096]{1,0:T(8,128)(2,1)S(1)}, bf16[64,4096]{1,0:T(8,128)(2,1)}, u32[]{:S(2)}) %copy-start) | copy-done | bytes 524312
  2.5 0.0 copy-start.1
  2.5 1.0 %copy-done.1 = bf16[512,512]{1,0:T(8,128)(2,1)S(1)} copy-done((bf16[512,512]{1,0:T(8,128)(2,1)S(1)}, bf16[512,512]{1,0:T(8,128)(2,1)}, u32[]{:S(2)}) %copy-start.1) | copy-done | bytes 524312
  3.6 0.0 copy-start.2
  3.6 0.9 %copy-done.2 = f32[64,512]{1,0:T(8,128)S(1)} copy-done((f32[64,512]{1,0:T(8,128)S(1)}, f32[64,512]{1,0:T(8,128)}, u32[]{:S(2)}) %copy-start.2) | copy-done | bytes 131096
  4.5 0.0 copy-start.3
  4.5 0.8 %copy-done.3 = bf16[3,4096]{1,0:T(4,128)(2,1)S(1)} copy-done((bf16[3,4096]{1,0:T(4,128)(2,1)S(1)}, bf16[3,4096]{1,0:T(4,128)(2,1)}, u32[]{:S(2)}) %copy-start.3) | copy-done | bytes 24600
  5.2 0.0 copy-start.4
  5.2 0.8 %copy-done.4 = f32[64,64]{1,0:T(8,128)S(1)} copy-done((f32[64,64]{1,0:T(8,128)S(1)}, f32[64,64]{1,0:T(8,128)}, u32[]{:S(2)}) %copy-start.4) | copy-done | bytes 16408
  6.0 0.0 copy-start.6
  6.0 0.7 %copy-done.6 = s32[8,64]{1,0:T(8,128)S(1)} copy-done((s32[8,64]{1,0:T(8,128)S(1)}, s32[8,64]{1,0:T(8,128)}, u32[]{:S(2)}) %copy-start.6) | copy-done | bytes 2072
  6.7 0.0 copy-start.7
  6.7 0.7 %copy-done.7 = s32[8,5]{1,0:T(8,128)S(1)} copy-done((s32[8,5]{1,0:T(8,128)S(1)}, s32[8,5]{1,0:T(8,128)}, u32[]{:S(2)}) %copy-start.7) | copy-done | bytes 184
  7.4 54.8 %shard_map.140 = (f32[64,4096]{1,0:T(8,128)S(1)}, f32[64,4096]{1,0:T(8,128)S(1)}) custom-call(bf16[64,4096]{1,0:T(8,128)(2,1)S(1)} %copy-done, bf16[3,4096]{1,0:T(4,128)(2,1)S(1)} %copy-done.3, bf16[512,512]{1,0:T(8,128)(2,1)S(1)} %copy-done.1, f32[64,512]{1,0:T(8,128)S(1)} %copy-done.2, f32[64,64]{1,0:T(8,128)S(1)} %copy-done.4, s32[8,64]{1,0:T(8,128)S(1)} %copy-done.5, ...), custom_call_target="tpu_custom_call" | custom-call | tf_op jit(solution)/shard_map/pallas_call | solution.py:550
  62.2 1.0 %copy.18 = f32[64,4096]{1,0:T(8,128)} copy(f32[64,4096]{1,0:T(8,128)S(1)} %get-tuple-element.4) | data formatting | bytes 2097152
  63.2 1.0 %copy.19 = f32[64,4096]{1,0:T(8,128)} copy(f32[64,4096]{1,0:T(8,128)S(1)} %get-tuple-element.5) | data formatting | bytes 2097152
Async XLA Ops:
  0.6 0.8 %copy-start.8 = (s32[1,64]{1,0:T(1,128)S(1)}, s32[1,64]{1,0:T(1,128)}, u32[]{:S(2)}) copy-start(s32[1,64]{1,0:T(1,128)} %dev_skel.1) | copy-start | bytes 772
  0.6 0.8 %copy-start.5 = (s32[8,64]{1,0:T(8,128)S(1)}, s32[8,64]{1,0:T(8,128)}, u32[]{:S(2)}) copy-start(s32[8,64]{1,0:T(8,128)} %leaf_skel.1) | copy-start | bytes 6148
  0.7 0.8 %copy-start.11 = (s32[1,2]{1,0:T(1,128)S(1)}, s32[1,2]{1,0:T(1,128)}, u32[]{:S(2)}) copy-start(s32[1,2]{1,0:T(1,128)} %oct_far.1) | copy-start | bytes 28
  0.7 0.8 %copy-start.10 = (s32[1,4]{1,0:T(1,128)S(1)}, s32[1,4]{1,0:T(1,128)}, u32[]{:S(2)}) copy-start(s32[1,4]{1,0:T(1,128)} %dev_far.1) | copy-start | bytes 52
  0.7 0.8 %copy-start.9 = (s32[8]{0:T(128)S(1)}, s32[8]{0:T(128)}, u32[]{:S(2)}) copy-start(s32[8]{0:T(128)} %near_count.1) | copy-start | bytes 100
  1.5 1.0 %copy-start = (bf16[64,4096]{1,0:T(8,128)(2,1)S(1)}, bf16[64,4096]{1,0:T(8,128)(2,1)}, u32[]{:S(2)}) copy-start(bf16[64,4096]{1,0:T(8,128)(2,1)} %probes.1) | copy-start | bytes 1572868
  2.5 1.0 %copy-start.1 = (bf16[512,512]{1,0:T(8,128)(2,1)S(1)}, bf16[512,512]{1,0:T(8,128)(2,1)}, u32[]{:S(2)}) copy-start(bf16[512,512]{1,0:T(8,128)(2,1)} %basis.1) | copy-start | bytes 1572868
  3.6 0.9 %copy-start.2 = (f32[64,512]{1,0:T(8,128)S(1)}, f32[64,512]{1,0:T(8,128)}, u32[]{:S(2)}) copy-start(f32[64,512]{1,0:T(8,128)} %dev_transfer.1) | copy-start | bytes 393220
  4.5 0.8 %copy-start.3 = (bf16[3,4096]{1,0:T(4,128)(2,1)S(1)}, bf16[3,4096]{1,0:T(4,128)(2,1)}, u32[]{:S(2)}) copy-start(bf16[3,4096]{1,0:T(4,128)(2,1)} %offsets.1) | copy-start | bytes 73732
  5.2 0.8 %copy-start.4 = (f32[64,64]{1,0:T(8,128)S(1)}, f32[64,64]{1,0:T(8,128)}, u32[]{:S(2)}) copy-start(f32[64,64]{1,0:T(8,128)} %oct_transfer.1) | copy-start | bytes 49156
  6.0 0.7 %copy-start.6 = (s32[8,64]{1,0:T(8,128)S(1)}, s32[8,64]{1,0:T(8,128)}, u32[]{:S(2)}) copy-start(s32[8,64]{1,0:T(8,128)} %oct_skel.1) | copy-start | bytes 6148
  6.7 0.7 %copy-start.7 = (s32[8,5]{1,0:T(8,128)S(1)}, s32[8,5]{1,0:T(8,128)}, u32[]{:S(2)}) copy-start(s32[8,5]{1,0:T(8,128)} %near_list.1) | copy-start | bytes 484

commit v2 on v1

--- a/solution.py
+++ b/solution.py
@@ -98,7 +98,21 @@
 def kernel(
     n_oct,
     n_leaf,
-    probes,
+    probes_in,
+    *refs,
+):
+    inputs, refs = refs[:12], refs[12:]
+    outputs, refs = refs[:2], refs[2:]
+    held, refs = refs[:12], refs[12:]
+    run(n_oct, n_leaf, probes_in, inputs, held, *held, *outputs, *refs)
+
+
+def run(
+    n_oct,
+    n_leaf,
+    probes_in,
+    inputs,
+    held,
     offsets,
     basis,
     dev_transfer,
@@ -113,6 +127,7 @@
     oct_far,
     out_value,
     out_slope,
+    load_sem,
     pext,
     oext,
     wq,
@@ -159,6 +174,21 @@
     def across(k):
         return lax.rem(o + k, n_oct)
 
+    loads = [
+        pltpu.make_async_copy(
+            probes_in.at[:, leaf * LEAF : (leaf + 1) * LEAF],
+            pext.at[WIN + leaf],
+            load_sem.at[leaf],
+        )
+        for leaf in range(LEAVES)
+    ]
+    loads += [
+        pltpu.make_async_copy(source, target, load_sem.at[LEAVES + i])
+        for i, (source, target) in enumerate(zip(inputs, held))
+    ]
+    for piece in loads:
+        piece.start()
+
     barrier = pltpu.get_barrier_semaphore()
 
     def greet(device):
@@ -179,12 +209,13 @@
 
     lax.fori_loop(1, n_oct, greet_across, 0)
 
+    for piece in loads:
+        piece.wait()
     base = box_corner(first)
     row512 = lax.broadcasted_iota(jnp.int32, (LEAF, SKEL), 0)
     charges, picked, corners = [], [], []
     for leaf in range(LEAVES):
         span = slice(leaf * LEAF, (leaf + 1) * LEAF)
-        pext[WIN + leaf] = probes[:, span]
         own = jnp.concatenate([offsets[:, span].astype(f32), jnp.zeros((5, LEAF), f32)], axis=0)
         oext[WIN + leaf] = own
         one_hot = jnp.where(row512 == leaf_skel[leaf : leaf + 1, :], 1.0, 0.0).astype(bf16)
@@ -253,7 +284,7 @@
         copy(wq.at[own], wq.at[0:LEAVES], halo_send.at[6], halo_recv.at[6], right_id),
         copy(wsk.at[own], wsk.at[0:LEAVES], halo_send.at[7], halo_recv.at[7], right_id),
     ]
-    for piece in halo:
+    for piece in halo[:4]:
         piece.start()
 
     def gather_copy(peer, slot):
@@ -262,8 +293,6 @@
     def gather_start(k, _):
         gather_copy(in_region(k), me).start()
         return 0
-
-    lax.fori_loop(1, n_leaf, gather_start, 0)
 
     row8 = lax.broadcasted_iota(jnp.int32, (8, LEAF), 0)
 
@@ -365,9 +394,59 @@
             ops += [upper, corner, lower]
         return ops
 
-    pipe(LEAVES, self_make, self_use)
-
-    for piece in halo:
+    def oct_copy(k, slot):
+        return copy(
+            tiles.at[0], regions.at[slot], oct_send.at[k], oct_recv.at[slot], (across(k), me)
+        )
+
+    def spread_copy(peer, slot):
+        return copy(chosen, spread.at[slot], spread_send.at[peer], spread_recv.at[slot], (o, peer))
+
+    def each(lo, hi, fn):
+        def step(k, _):
+            fn(k)
+            return 0
+
+        lax.fori_loop(lo, hi, step, 0)
+
+    def sum_region():
+        @pl.when(me < RED)
+        def _():
+            each(1, n_leaf, lambda k: reduce_copy(0, in_region(k)).wait_recv())
+            for t in range(RED):
+
+                @pl.when(me != t)
+                def _():
+                    reduce_copy(t, me).wait_send()
+
+            total = jnp.sum(gathered[...], axis=0)
+            regions[o] = total
+            tiles[0] = total
+            each(1, n_oct, lambda k: oct_copy(k, o).start())
+
+    def spread_regions():
+        @pl.when(me < RED)
+        def _():
+            each(1, n_oct, lambda k: oct_copy(k, across(k)).wait_recv())
+            one, two = [regions[inside(oct_far[0, i], n_oct)] for i in range(2)]
+            pair_of = jnp.concatenate([one[:, :SKEL], two[:, :SKEL]], axis=1)
+            mine = jnp.concatenate([regions[o][:3], regions[o][:3], regions[o][:2]], axis=0)
+            row = lax.broadcasted_iota(jnp.int32, (8, 2 * SKEL), 0)
+            message = jnp.where((row >= 3) & (me == RED - 1), mine, pair_of)
+            chosen[...] = message
+            spread[me] = message
+            each(1, n_leaf, lambda k: spread_copy(in_region(k), me).start())
+
+        for piece in halo[4:]:
+            piece.start()
+        lax.fori_loop(1, n_leaf, gather_start, 0)
+
+    def between_self(k):
+        pl.when(k == 2)(sum_region)
+
+    pipe(LEAVES, self_make, self_use, between_self)
+
+    for piece in halo[:4]:
         piece.wait_recv()
     for e in list(range(WIN)) + list(range(WIN + LEAVES, EXT)):
         leaf = lax.rem(first + devices * LEAVES + e - WIN, devices * LEAVES)
@@ -402,50 +481,8 @@
                 ops += [forward, back]
         return ops
 
-    def oct_copy(k, slot):
-        return copy(
-            tiles.at[0], regions.at[slot], oct_send.at[k], oct_recv.at[slot], (across(k), me)
-        )
-
-    def spread_copy(peer, slot):
-        return copy(chosen, spread.at[slot], spread_send.at[peer], spread_recv.at[slot], (o, peer))
-
-    def each(lo, hi, fn):
-        def step(k, _):
-            fn(k)
-            return 0
-
-        lax.fori_loop(lo, hi, step, 0)
-
-    def sum_region():
-        @pl.when(me < RED)
-        def _():
-            each(1, n_leaf, lambda k: reduce_copy(0, in_region(k)).wait_recv())
-            for t in range(RED):
-
-                @pl.when(me != t)
-                def _():
-                    reduce_copy(t, me).wait_send()
-
-            total = jnp.sum(gathered[...], axis=0)
-            regions[o] = total
-            tiles[0] = total
-            each(1, n_oct, lambda k: oct_copy(k, o).start())
-
-    def spread_regions():
-        @pl.when(me < RED)
-        def _():
-            each(1, n_oct, lambda k: oct_copy(k, across(k)).wait_recv())
-            one, two = [regions[inside(oct_far[0, i], n_oct)] for i in range(2)]
-            message = [jnp.concatenate([one[:, :SKEL], two[:, :SKEL]], axis=1), regions[o]]
-            for m in range(2):
-                chosen[m] = message[m]
-                spread[me, m] = message[m]
-            each(1, n_leaf, lambda k: spread_copy(in_region(k), me).start())
-
     def between(k):
-        pl.when(k == 1)(sum_region)
-        pl.when(k == 4)(spread_regions)
+        pl.when(k == 2)(spread_regions)
 
     pipe(19, pair_make, pair_use, between)
 
@@ -458,6 +495,9 @@
         for axis in range(3):
             at = 8 * leaf + axis
             columns[leaf, axis] = jnp.broadcast_to(upright[:, at : at + 1], wide)
+
+    for piece in halo[4:]:
+        piece.wait_recv()
 
     def leaf_field(leaf, _):
         targets = [columns[leaf, axis] for axis in range(3)]
@@ -494,12 +534,12 @@
         def _():
             spread_copy(t, t).wait_recv()
 
-    charge = spread[0 : RED - 1, 0].reshape(PROBES, 2 * SKEL)
-    source = spread[RED - 1, 0]
+    charge = spread[0 : RED - 1].reshape(PROBES, 2 * SKEL)
+    source = spread[RED - 1]
     upright = jnp.transpose(
-        jnp.concatenate([spread[RED - 1, 1], jnp.zeros((120, 2 * SKEL), f32)], axis=0)
+        jnp.concatenate([source, jnp.zeros((120, 2 * SKEL), f32)], axis=0)
     )
-    targets = [upright[:SKEL, axis : axis + 1] for axis in range(3)]
+    targets = [upright[:SKEL, 3 + axis : 4 + axis] for axis in range(3)]
     oct_sum = dot3(charge, far_tile(targets, source), NT)
     down_dev = dot3(stacked(oct_sum), oct_transfer[...]) + stacked(dev_sum)
     down = dot3(down_dev, dev_transfer[...])
@@ -543,16 +583,29 @@
         oct_skel,
     ) = args
     vmem = pl.BlockSpec(memory_space=pltpu.VMEM)
-    smem = pl.BlockSpec(memory_space=pltpu.SMEM)
+    hbm = pl.BlockSpec(memory_space=pltpu.HBM)
     points = probes.shape[1]
+    in_vmem = (
+        offsets,
+        leaf_basis,
+        dev_transfer,
+        oct_transfer,
+        leaf_skel,
+        dev_skel,
+        oct_skel,
+    )
+    in_smem = (near_list, near_count, leaf_far, dev_far, oct_far)
     dma = pltpu.SemaphoreType.DMA
     out = jax.ShapeDtypeStruct((PROBES, points), f32)
     return pl.pallas_call(
         functools.partial(kernel, n_oct, n_leaf),
         out_shape=(out, out),
-        in_specs=[vmem] * 8 + [smem] * 5,
+        in_specs=[hbm] * 13,
         out_specs=(vmem, vmem),
         scratch_shapes=[
+            *[pltpu.VMEM(v.shape, v.dtype) for v in in_vmem],
+            *[pltpu.SMEM(v.shape, v.dtype) for v in in_smem],
+            dma((LEAVES + 12,)),
             pltpu.VMEM((EXT, PROBES, LEAF), bf16),
             pltpu.VMEM((EXT, 8, LEAF), f32),
             pltpu.VMEM((WIDE, PROBES, 2 * SKEL), bf16),
@@ -561,8 +614,8 @@
             pltpu.VMEM((RED, 8, 2 * SKEL), f32),
             pltpu.VMEM((n_leaf, 8, 2 * SKEL), f32),
             pltpu.VMEM((n_oct, 8, 2 * SKEL), f32),
-            pltpu.VMEM((2, 8, 2 * SKEL), f32),
-            pltpu.VMEM((RED, 2, 8, 2 * SKEL), f32),
+            pltpu.VMEM((8, 2 * SKEL), f32),
+            pltpu.VMEM((RED, 8, 2 * SKEL), f32),
             pltpu.VMEM((EXT, LEAF, FEAT), bf16),
             pltpu.VMEM((EXT, FEAT, LEAF), bf16),
             pltpu.VMEM((LEAF, LEAF), bf16),
@@ -584,23 +637,9 @@
             dma((n_leaf,)),
         ],
         compiler_params=pltpu.CompilerParams(
-            collective_id=0, has_side_effects=True, vmem_limit_bytes=48 * 2**20
+            collective_id=0, has_side_effects=True, vmem_limit_bytes=60 * 2**20
         ),
-    )(
-        probes,
-        offsets,
-        leaf_basis,
-        dev_transfer,
-        oct_transfer,
-        leaf_skel,
-        dev_skel,
-        oct_skel,
-        near_list,
-        near_count,
-        leaf_far,
-        dev_far,
-        oct_far,
-    )
+    )(probes, *in_vmem, *in_smem)
 
 
 def solution(mesh):

time: 64.6 us -> 55 us (0.85)
  Pallas kernels: 54.8 us -> 49.5 us
  local copies, waits for them, and re-layouts: 8.62 us -> 4.68 us
    pallas_call x1, Pallas kernels: 54.8 us -> 49.5 us  [body(): pl.pallas_call(functools.partial(kernel, n_oct, n_leaf), out_shape=(out,...]
    unnamed x27 -> x5, local copies, waits for them, and re-layouts: 8.62 us -> 4.68 us
where the time goes in v2:
time: 55 us; the launch traced here: 54.8 us
  Pallas kernels  49.5 us (90%)
  local copies, waits for them, and re-layouts  4.68 us (9%)
  between operations  0.65 us (1%)
    pallas_call x1, Pallas kernels, body(): pl.pallas_call(functools.partial(kernel, n_oct, n_leaf), out_shape=(out,...  49.5 us
    unnamed x5, local copies, waits for them, and re-layouts  4.68 us

profile of v2, /device:TPU:1, one launch (start us, length us, event | category | flops | bytes accessed | tf_op | source)
XLA Modules:
  0.0 54.8 jit_solution(9343876754954716458)
XLA Ops:
  0.6 1.3 %copy.15.refs_9_ = s32[8,4]{1,0:T(8,128)} copy(s32[8,4]{0,1:T(4,128)} %param.20) | data formatting | bytes 256 | tf_op args[7]
  2.0 49.5 %shard_map.140 = (f32[64,4096]{1,0:T(8,128)}, f32[64,4096]{1,0:T(8,128)}) custom-call(bf16[64,4096]{1,0:T(8,128)(2,1)} %probes_in.1, bf16[3,4096]{1,0:T(4,128)(2,1)} %refs_0_.1, bf16[512,512]{1,0:T(8,128)(2,1)} %refs_1_.1, f32[64,512]{1,0:T(8,128)} %refs_2_.1, f32[64,64]{1,0:T(8,128)} %refs_3_.1, s32[8,64]{1,0:T(8,128)} %refs_4_.1, s32[1,64]{1,0:T(1,128)} %refs_5_.1, ...), custom_call_target="tpu_custom_call" | custom-call | tf_op jit(solution)/shard_map/pallas_call | solution.py:600
  51.5 0.0 copy-start
  51.5 2.4 %copy.18 = f32[64,4096]{1,0:T(8,128)} copy(f32[64,4096]{1,0:T(8,128)} %get-tuple-element.4) | data formatting | bytes 2097152
  53.9 0.0 copy-done
  53.9 1.0 %copy.19 = f32[64,4096]{1,0:T(8,128)} copy(f32[64,4096]{1,0:T(8,128)S(1)} %copy-done) | data formatting | bytes 2097152
Async XLA Ops:
  51.5 2.4 %copy-start = (f32[64,4096]{1,0:T(8,128)S(1)}, f32[64,4096]{1,0:T(8,128)}, u32[]{:S(2)}) copy-start(f32[64,4096]{1,0:T(8,128)} %get-tuple-element.5) | copy-start | bytes 3145732

commit v3 on v2

--- a/solution.py
+++ b/solution.py
@@ -246,6 +246,106 @@
         tiles[t] = jnp.concatenate([upward[8 * t : 8 * t + 8], blank], axis=1)
     tiles[RED - 1] = jnp.concatenate([oct_both[:8] + oct_both[8:], blank], axis=1)
 
+    row8 = lax.broadcasted_iota(jnp.int32, (8, LEAF), 0)
+
+    def features(e, corner):
+        off = oext[e]
+        anchor = rows_of(corner, (8, LEAF))
+        pos = off + anchor
+        norm = split3(jnp.sum(pos * pos, axis=0, keepdims=True) * (1.0 / 12.0))
+        parts = split3(pos * (-1.0 / 6.0))
+
+        def mixed(at):
+            v = jnp.zeros((8, LEAF), f32)
+            for i in range(3):
+                v = jnp.where(row8 == at + i, norm[i], v)
+            return jnp.where((row8 >= 3 - at) & (row8 < 6 - at), 1.0, v)
+
+        pad = jnp.zeros((8, LEAF), f32)
+        rows_f = jnp.concatenate([*parts, *parts, mixed(0), pad], axis=0)
+        feat_f[e] = jnp.transpose(rows_f).astype(bf16)
+        rows_g = jnp.concatenate([anchor] * 3 + [off] * 3 + [mixed(3), pad], axis=0)
+        feat_g[e] = rows_g.astype(bf16)
+
+    for leaf in range(LEAVES):
+        features(WIN + leaf, [leaf & 1, leaf >> 1 & 1, leaf >> 2 & 1])
+
+    def uses(target, source):
+        leaf = lax.rem(target + LEAVES - WIN, LEAVES)
+        wanted_leaf = first + source - WIN
+        count = near_count[leaf]
+        total = jnp.float32(0.0)
+        for s in range(near_list.shape[1]):
+            hit = (near_list[leaf, s] == wanted_leaf) & (s < count)
+            total = total + jnp.where(hit, jnp.float32(1.0), jnp.float32(0.0))
+        return total
+
+    def tile(a, b, kv, ks, rows, cols):
+        value, slope = matern(dot(feat_f[a, rows, :], feat_g[b, :, cols]))
+        kv[rows, cols] = value.astype(bf16)
+        ks[rows, cols] = slope.astype(bf16)
+
+    def interleave(first_ops, second_ops):
+        done = 0
+        for i, op in enumerate(first_ops):
+            op()
+            upto = (i + 1) * len(second_ops) // len(first_ops)
+            for q in range(done, upto):
+                second_ops[q]()
+            done = upto
+
+    def pipe(n, make, use, between=lambda k: None):
+        bufs = ((kv0, ks0), (kv1, ks1))
+        for op in make(0, *bufs[0]):
+            op()
+        steps = (n - 1) // 2
+
+        def body(k, _):
+            between(k)
+            interleave(make(2 * k + 1, *bufs[1]), use(2 * k, *bufs[0]))
+            interleave(make(2 * k + 2, *bufs[0]), use(2 * k + 1, *bufs[1]))
+            return 0
+
+        lax.fori_loop(0, steps, body, 0)
+        if n % 2:
+            for op in use(n - 1, *bufs[0]):
+                op()
+        else:
+            interleave(make(n - 1, *bufs[1]), use(n - 2, *bufs[0]))
+            for op in use(n - 1, *bufs[1]):
+                op()
+
+    half = LEAF // 2
+    low, high, full = slice(0, half), slice(half, LEAF), slice(0, LEAF)
+
+    def self_make(i, kv, ks):
+        e = i + WIN
+        ops = []
+        for r in range(0, LEAF, 64):
+            cols = full if r < half else high
+            ops.append(lambda r=r, cols=cols: tile(e, e, kv, ks, slice(r, r + 64), cols))
+        return ops
+
+    def self_use(i, kv, ks):
+        e = i + WIN
+        c = uses(e, e)
+        ops = []
+        for m, k in enumerate((kv, ks)):
+
+            def upper(m=m, k=k):
+                acc[e, m] = c * dot(pext[e, :, low], k[low, :])
+
+            def corner(m=m, k=k):
+                acc[e, m, :, high] += c * dot(pext[e, :, high], k[high, high])
+
+            def lower(m=m, k=k):
+                acc[e, m, :, low] += c * dot(pext[e, :, high], k[low, high], NT)
+
+            ops += [upper, corner, lower]
+        return ops
+
+    pipe(LEAVES, self_make, self_use)
+
     pl.semaphore_wait(barrier, n_leaf - 1 + n_oct - 1 + 2)
 
     def copy(src, dst, send, recv, device):
@@ -294,105 +394,6 @@
         gather_copy(in_region(k), me).start()
         return 0
 
-    row8 = lax.broadcasted_iota(jnp.int32, (8, LEAF), 0)
-
-    def features(e, corner):
-        off = oext[e]
-        anchor = rows_of(corner, (8, LEAF))
-        pos = off + anchor
-        norm = split3(jnp.sum(pos * pos, axis=0, keepdims=True) * (1.0 / 12.0))
-        parts = split3(pos * (-1.0 / 6.0))
-
-        def mixed(at):
-            v = jnp.zeros((8, LEAF), f32)
-            for i in range(3):
-                v = jnp.where(row8 == at + i, norm[i], v)
-            return jnp.where((row8 >= 3 - at) & (row8 < 6 - at), 1.0, v)
-
-        pad = jnp.zeros((8, LEAF), f32)
-        rows_f = jnp.concatenate([*parts, *parts, mixed(0), pad], axis=0)
-        feat_f[e] = jnp.transpose(rows_f).astype(bf16)
-        rows_g = jnp.concatenate([anchor] * 3 + [off] * 3 + [mixed(3), pad], axis=0)
-        feat_g[e] = rows_g.astype(bf16)
-
-    for leaf in range(LEAVES):
-        features(WIN + leaf, [leaf & 1, leaf >> 1 & 1, leaf >> 2 & 1])
-    for e in range(EXT):
-        acc[e] = jnp.zeros((2, PROBES, LEAF), f32)
-
-    def uses(target, source):
-        leaf = lax.rem(target + LEAVES - WIN, LEAVES)
-        wanted_leaf = first + source - WIN
-        count = near_count[leaf]
-        total = jnp.float32(0.0)
-        for s in range(near_list.shape[1]):
-            hit = (near_list[leaf, s] == wanted_leaf) & (s < count)
-            total = total + jnp.where(hit, jnp.float32(1.0), jnp.float32(0.0))
-        return total
-
-    def tile(a, b, kv, ks, rows, cols):
-        value, slope = matern(dot(feat_f[a, rows, :], feat_g[b, :, cols]))
-        kv[rows, cols] = value.astype(bf16)
-        ks[rows, cols] = slope.astype(bf16)
-
-    def interleave(first_ops, second_ops):
-        done = 0
-        for i, op in enumerate(first_ops):
-            op()
-            upto = (i + 1) * len(second_ops) // len(first_ops)
-            for q in range(done, upto):
-                second_ops[q]()
-            done = upto
-
-    def pipe(n, make, use, between=lambda k: None):
-        bufs = ((kv0, ks0), (kv1, ks1))
-        for op in make(0, *bufs[0]):
-            op()
-        steps = (n - 1) // 2
-
-        def body(k, _):
-            between(k)
-            interleave(make(2 * k + 1, *bufs[1]), use(2 * k, *bufs[0]))
-            interleave(make(2 * k + 2, *bufs[0]), use(2 * k + 1, *bufs[1]))
-            return 0
-
-        lax.fori_loop(0, steps, body, 0)
-        if n % 2:
-            for op in use(n - 1, *bufs[0]):
-                op()
-        else:
-            interleave(make(n - 1, *bufs[1]), use(n - 2, *bufs[0]))
-            for op in use(n - 1, *bufs[1]):
-                op()
-
-    half = LEAF // 2
-    low, high, full = slice(0, half), slice(half, LEAF), slice(0, LEAF)
-
-    def self_make(i, kv, ks):
-        e = i + WIN
-        ops = []
-        for r in range(0, LEAF, 64):
-            cols = full if r < half else high
-            ops.append(lambda r=r, cols=cols: tile(e, e, kv, ks, slice(r, r + 64), cols))
-        return ops
-
-    def self_use(i, kv, ks):
-        e = i + WIN
-        c = uses(e, e)
-        ops = []
-        for m, k in enumerate((kv, ks)):
-
-            def upper(m=m, k=k):
-                acc[e, m] = c * dot(pext[e, :, low], k[low, :])
-
-            def corner(m=m, k=k):
-                acc[e, m, :, high] += c * dot(pext[e, :, high], k[high, high])
-
-            def lower(m=m, k=k):
-                acc[e, m, :, low] += c * dot(pext[e, :, high], k[low, high], NT)
-
-            ops += [upper, corner, lower]
-        return ops
 
     def oct_copy(k, slot):
         return copy(
@@ -437,25 +438,10 @@
             spread[me] = message
             each(1, n_leaf, lambda k: spread_copy(in_region(k), me).start())
 
-        for piece in halo[4:]:
-            piece.start()
-        lax.fori_loop(1, n_leaf, gather_start, 0)
-
-    def between_self(k):
-        pl.when(k == 2)(sum_region)
-
-    pipe(LEAVES, self_make, self_use, between_self)
-
-    for piece in halo[:4]:
-        piece.wait_recv()
-    for e in list(range(WIN)) + list(range(WIN + LEAVES, EXT)):
-        leaf = lax.rem(first + devices * LEAVES + e - WIN, devices * LEAVES)
-        there = box_corner(leaf)
-        features(e, [there[i] - base[i] for i in range(3)])
 
     def pair(i):
-        s = (i + 1) // 10
-        a = i + 1 - 10 * s
+        s = i // 7
+        a = i + WIN - 7 * s
         return a, a + 1 + s
 
     def pair_make(i, kv, ks):
@@ -481,10 +467,52 @@
                 ops += [forward, back]
         return ops
 
+    def bulk():
+        for piece in halo[4:]:
+            piece.start()
+        lax.fori_loop(1, n_leaf, gather_start, 0)
+
     def between(k):
-        pl.when(k == 2)(spread_regions)
-
-    pipe(19, pair_make, pair_use, between)
+        pl.when(k == 2)(sum_region)
+        pl.when(k == 2)(bulk)
+        pl.when(k == 4)(spread_regions)
+
+    pipe(13, pair_make, pair_use, between)
+
+    for piece in halo[:4]:
+        piece.wait_recv()
+    for e in list(range(WIN)) + list(range(WIN + LEAVES, EXT)):
+        leaf = lax.rem(first + devices * LEAVES + e - WIN, devices * LEAVES)
+        there = box_corner(leaf)
+        features(e, [there[i] - base[i] for i in range(3)])
+
+    def edge(i):
+        r = i % 3
+        source, target = 1 - r % 2, 2 + r // 2
+        side = i // 3
+        last = EXT - 1
+        return source + side * (last - 2 * source), target + side * (last - 2 * target)
+
+    def edge_make(i, kv, ks):
+        a, b = edge(i)
+        return [
+            lambda r=r: tile(a, b, kv, ks, slice(r, r + 64), full) for r in range(0, LEAF, 64)
+        ]
+
+    def edge_use(i, kv, ks):
+        a, b = edge(i)
+        c = uses(b, a)
+        ops = []
+        for m, k in enumerate((kv, ks)):
+            for span in (low, high):
+
+                def forward(m=m, k=k, span=span):
+                    acc[b, m, :, span] += c * dot(pext[a], k[:, span])
+
+                ops.append(forward)
+        return ops
+
+    pipe(6, edge_make, edge_use)
 
     upright = jnp.concatenate(
         [wsk[LEAVES + leaf] for leaf in range(LEAVES)] + [dev_pos] + [blank] * 7, axis=0
@@ -514,7 +542,7 @@
         far_sum[leaf] = total
         return 0
 
-    lax.fori_loop(0, LEAVES, leaf_field, 0)
+    lax.fori_loop(0, LEAVES, leaf_field, 0, unroll=4)
 
     each(1, n_leaf, lambda k: gather_copy(me, in_region(k)).wait_recv())
     targets = [columns[LEAVES, axis] for axis in range(3)]

time: 55 us -> 50.3 us (0.915)
  Pallas kernels: 49.5 us -> 44.9 us
    pallas_call x1, Pallas kernels: 49.5 us -> 44.9 us  [body(): pl.pallas_call(functools.partial(kernel, n_oct, n_leaf), out_shape=(out,...]
where the time goes in v3:
time: 50.3 us; the launch traced here: 50.2 us
  Pallas kernels  44.9 us (89%)
  local copies, waits for them, and re-layouts  4.68 us (9%)
  between operations  0.65 us (1%)
    pallas_call x1, Pallas kernels, body(): pl.pallas_call(functools.partial(kernel, n_oct, n_leaf), out_shape=(out,...  44.9 us
    unnamed x5, local copies, waits for them, and re-layouts  4.68 us

profile of v3, /device:TPU:1, one launch (start us, length us, event | category | flops | bytes accessed | tf_op | source)
XLA Modules:
  0.0 50.2 jit_solution(7801446699132980954)
XLA Ops:
  0.6 1.3 %copy.15.refs_9_ = s32[8,4]{1,0:T(8,128)} copy(s32[8,4]{0,1:T(4,128)} %param.20) | data formatting | bytes 256 | tf_op args[7]
  2.0 44.9 %shard_map.140 = (f32[64,4096]{1,0:T(8,128)}, f32[64,4096]{1,0:T(8,128)}) custom-call(bf16[64,4096]{1,0:T(8,128)(2,1)} %probes_in.1, bf16[3,4096]{1,0:T(4,128)(2,1)} %refs_0_.1, bf16[512,512]{1,0:T(8,128)(2,1)} %refs_1_.1, f32[64,512]{1,0:T(8,128)} %refs_2_.1, f32[64,64]{1,0:T(8,128)} %refs_3_.1, s32[8,64]{1,0:T(8,128)} %refs_4_.1, s32[1,64]{1,0:T(1,128)} %refs_5_.1, ...), custom_call_target="tpu_custom_call" | custom-call | tf_op jit(solution)/shard_map/pallas_call | solution.py:628
  46.8 0.0 copy-start
  46.8 2.4 %copy.18 = f32[64,4096]{1,0:T(8,128)} copy(f32[64,4096]{1,0:T(8,128)} %get-tuple-element.4) | data formatting | bytes 2097152
  49.2 0.0 copy-done
  49.2 1.0 %copy.19 = f32[64,4096]{1,0:T(8,128)} copy(f32[64,4096]{1,0:T(8,128)S(1)} %copy-done) | data formatting | bytes 2097152
Async XLA Ops:
  46.8 2.4 %copy-start = (f32[64,4096]{1,0:T(8,128)S(1)}, f32[64,4096]{1,0:T(8,128)}, u32[]{:S(2)}) copy-start(f32[64,4096]{1,0:T(8,128)} %get-tuple-element.5) | copy-start | bytes 3145732
